TPU v7x, 32 devices: a whole 2x2x4 slice. The times are simulated.
32 devices in a mesh: slab: 2 (over x), plane: 8 (over z, y), brick: 2 (over core).
Axes of the slice: x: 2, y: 2, z: 4, core: 2. Of those that a mesh axis runs over, the one named last changes fastest.
Arguments:
- camera_rows: bfloat16 [4, 16, 32, 2048], P(None, 'slab', ('plane', 'brick')), parts along dimension 1, may hold values from 0.19921875 to 5
- estimate: float32 [16, 32, 2048], P('slab', None, ('plane', 'brick')), parts along dimension 0, may hold values from 0.2 to 5
- psf_bank: float32 [32, 4, 3, 31], P(('slab', 'plane', 'brick')), parts along dimension 0, may hold values from 0 to 1.25, as said below
- psf_owner: int32 [32], P('slab'), parts along dimension 0, may hold values from 0 to 15, each once
- view_mask: int32 [32, 4], P('slab'), parts along dimension 0, may hold values 0 or 1
Outputs:
- deconvolved: float32 [16, 32, 2048], P('slab', None, ('plane', 'brick')), parts along dimension 0
There are 2 independent parts, one for each index of `slab`. A program takes and returns all parts, laid end to end along the dimension named above; each array names one. Nothing has to cross between parts.
Inputs may be any that keep to these rules, and one draw needn't show every extreme that they name: `psf_owner`: every brick names a different device: the map is a permutation of 0 to 15. `psf_bank`: every tap is positive.
All inputs are finite; a program needn't handle non-finite values.
Results may differ from a plain program's by a relative error of at most 0.0003.
Values may be sent and summed in bfloat16 or wider, within the bound.
A program may use at most 192 MiB of HBM per device.

v0:
```python
import jax
import jax.numpy as jnp
from jax import lax
from jax.sharding import PartitionSpec as P

V = 4
RADIUS = 15
ITERS = 2
BACKGROUND = 0.1
HIGHEST = lax.Precision.HIGHEST


def padded_2(cells, sides, width):
    for axis, dim in sides:
        count = lax.axis_size(axis)
        ends = count - 1
        head = lax.slice_in_dim(cells, 0, width, axis=dim)
        tail = lax.slice_in_dim(cells, cells.shape[dim] - width, cells.shape[dim], axis=dim)
        cells = jnp.concatenate(
            [
                lax.ppermute(tail, axis, [(i, (i + 1) % count) for i in range(ends)]),
                cells,
                lax.ppermute(head, axis, [((i + 1) % count, i) for i in range(ends)]),
            ],
            axis=dim,
        )
    return cells


def banded(profiles, size_in, size_out, offset):
    tap_count = profiles.shape[-1]
    centre = tap_count // 2
    lag_index = (
        jnp.arange(size_in, dtype=jnp.int32)[:, None]
        - jnp.arange(size_out, dtype=jnp.int32)[None, :]
        - offset
        + centre
    )
    one_hot = (
        lag_index[:, :, None] == jnp.arange(tap_count, dtype=jnp.int32)[None, None, :]
    ).astype(jnp.float32)
    return jnp.einsum("ijt,vt->vij", one_hot, profiles, precision=HIGHEST)


def across_columns(volume, band_x):
    if volume.ndim == 3:
        return jnp.einsum("zyi,vij->vzyj", volume, band_x, precision=HIGHEST)
    return jnp.einsum("vzyi,vij->vzyj", volume, band_x, precision=HIGHEST)


def across_rows(volume, band_y):
    view_count, depth_count, row_count, col_count = volume.shape
    block_rows = band_y.shape[2]
    margin = (band_y.shape[1] - block_rows) // 2
    pieces = volume.reshape(view_count, depth_count, row_count // block_rows, block_rows, col_count)
    blanks = jnp.zeros((view_count, depth_count, 1, margin, col_count), jnp.float32)
    before = jnp.concatenate([blanks, pieces[:, :, :-1, block_rows - margin :, :]], axis=2)
    behind = jnp.concatenate([pieces[:, :, 1:, :margin, :], blanks], axis=2)
    windows = jnp.concatenate([before, pieces, behind], axis=3)
    result = jnp.einsum("vzqic,vij->vzqjc", windows, band_y, precision=HIGHEST)
    return result.reshape(view_count, depth_count, row_count, col_count)


def across_depth(volume, band_z):
    return jnp.einsum("vzyc,vzw->vwyc", volume, band_z, precision=HIGHEST)


def separable(volume, bands):
    return across_depth(across_rows(across_columns(volume, bands[0]), bands[1]), bands[2])


def shards(camera_rows, estimate, psf_bank, psf_owner, view_mask):
    regrouped = lax.all_to_all(
        camera_rows, ("plane", "brick"), split_axis=3, concat_axis=2, tiled=True
    )
    position = lax.axis_index(("plane", "brick"))
    brick_ids = jnp.arange(psf_owner.shape[0], dtype=jnp.int32)
    is_mine = brick_ids == position
    owner_id = jnp.sum(jnp.where(is_mine, psf_owner, 0))
    observed = jnp.sum(jnp.where(is_mine[:, None], view_mask, 0), axis=0) > 0
    fitted = lax.all_gather(psf_bank, ("plane", "brick"), axis=0, tiled=True)
    chosen = (brick_ids == owner_id).astype(jnp.float32)
    kernels = jnp.einsum("b,bvat->vat", chosen, fitted, precision=HIGHEST)
    kernels = kernels / jnp.sum(kernels, axis=-1, keepdims=True)
    flipped = kernels[:, :, ::-1]
    depth_size = estimate.shape[0]
    row_size = estimate.shape[1]
    col_size = estimate.shape[2]
    block_size = 128 if row_size % 128 == 0 else row_size

    def make_bands(profiles):
        return (
            banded(profiles[:, 2], col_size + 2 * RADIUS, col_size, RADIUS),
            banded(profiles[:, 1], block_size + 2 * RADIUS, block_size, RADIUS),
            banded(profiles[:, 0], depth_size, depth_size, 0),
        )

    blur_bands = make_bands(kernels)
    back_bands = make_bands(flipped)
    current = estimate
    for iteration in range(ITERS):
        padded = padded_2(current.astype(jnp.bfloat16), ((("plane", "brick"), 2),), RADIUS).astype(
            current.dtype
        )
        blurred = separable(padded, blur_bands)
        quotient = jnp.where(
            observed[:, None, None, None],
            regrouped.astype(jnp.float32) / (blurred + BACKGROUND),
            0.0,
        )
        quotient_wide = padded_2(
            quotient.astype(jnp.bfloat16), ((("plane", "brick"), 3),), RADIUS
        ).astype(quotient.dtype)
        corrected = separable(quotient_wide, back_bands)
        factor = jnp.sum(jnp.where(observed[:, None, None, None], corrected, 1.0), axis=0) / V
        current = current * factor
    return current


def solution(mesh):
    return jax.shard_map(
        shards,
        mesh=mesh,
        in_specs=(
            P(None, "slab", ("plane", "brick"), None),
            P("slab", None, ("plane", "brick")),
            P(("slab", "plane", "brick"), None, None, None),
            P("slab"),
            P("slab", None),
        ),
        out_specs=P("slab", None, ("plane", "brick")),
        check_vma=False,
    )
```

profile of v0, /device:TPU:1, one launch (start us, length us, event | category | flops | bytes accessed | tf_op | source)
XLA Modules:
  0.0 100.3 jit_solution(6253015987272240798)
XLA Ops:
  0.0 6.3 %copy.47 = bf16[4,8,2,2048]{1,0,2,3:T(4,128)(2,1)} copy(bf16[4,8,2,2048]{3,2,1,0:T(2,128)(2,1)} %param.5) | data formatting | bytes 524288 | tf_op args[0]
  6.3 0.0 copy-start
  6.3 0.0 copy-start.1
  6.4 6.5 %reshape.127 = bf16[16,2,4096]{2,1,0:T(2,128)(2,1)} reshape(bf16[2048,2,4,8]{3,2,1,0:T(4,128)(2,1)} %bitcast.116) | data formatting | bytes 524288
  12.8 7.3 %all-to-all-start = ((bf16[16,2,4096]{2,1,0:T(2,128)(2,1)}), bf16[16,2,4096]{2,1,0:T(2,128)(2,1)S(1)}, u32[]{:S(2)}, u32[]{:S(2)}) async-start(bf16[16,2,4096]{2,1,0:T(2,128)(2,1)} %reshape.127), calls=%async_computation | async-start | bytes 524288 | tf_op jit(solution)/shard_map/all_to_all | solution.py:73
  20.2 0.0 copy-done
  20.2 0.1 fusion.79
  20.3 2.0 %collective-permute-start.1 = (bf16[8,32,15]{2,1,0:T(8,128)(2,1)S(1)}, bf16[8,32,15]{2,1,0:T(8,128)(2,1)S(1)}, u32[]{:S(2)}, u32[]{:S(2)}) collective-permute-start(bf16[8,32,15]{2,1,0:T(8,128)(2,1)S(1)} %get-tuple-element.12), channel_id=1, source_target_pairs={{1,0},{2,1},{3,2},{4,3},{5,4},{6,5},{7,6},{8,7},{9,8},{10,9},{11,1... | collective-permute-start | bytes 23048 | tf_op jit(solution)/shard_map/ppermute | solution.py:23
  22.3 3.5 %collective-permute-start = (bf16[8,32,15]{2,1,0:T(8,128)(2,1)S(1)}, bf16[8,32,15]{2,1,0:T(8,128)(2,1)S(1)}, u32[]{:S(2)}, u32[]{:S(2)}) collective-permute-start(bf16[8,32,15]{2,1,0:T(8,128)(2,1)S(1)} %get-tuple-element.11), channel_id=1, source_target_pairs={{0,1},{1,2},{2,3},{3,4},{4,5},{5,6},{6,7},{7,8},{8,9},{9,10},{10,1... | collective-permute-start | bytes 23048 | tf_op jit(solution)/shard_map/ppermute | solution.py:21
  25.9 0.0 copy-done.1
  25.9 20.7 %all_gather.3 = f32[16,4,3,31]{3,1,2,0:T(4,128)S(1)} all-gather(f32[1,4,3,31]{3,1,2,0:T(4,128)S(1)} %copy-done.1), channel_id=1, replica_groups=mesh['slab'=2,'plane'=8,'brick'=2] {'plane','brick'}, dimensions={0}, use_global_device_ids=true | all-gather | bytes 25296 | tf_op jit(solution)/shard_map/all_gather | solution.py:81
  46.6 0.0 copy-done.3
  46.6 0.6 select_reduce_fusion.1
  47.2 0.8 fusion.48
  48.0 0.1 bitcast_reduce_fusion
  48.1 0.1 bitcast_divide_fusion
  48.2 0.9 fusion.12
  49.1 0.3 convolution_bitcast_fusion.8
  49.4 0.0 copy-done.2
  49.4 0.1 select_reduce_fusion
  49.5 0.1 slice.54
  49.6 0.9 fusion.13
  50.5 0.1 slice.48
  50.6 0.3 convolution_bitcast_fusion.9
  50.9 0.4 convolution_bitcast_fusion.10
  51.3 0.1 slice.46
  51.4 0.1 copy.74
  51.5 0.0 collective-permute-done.1
  51.5 0.0 collective-permute-done
  51.5 0.5 convolution_bitcast_fusion.1
  52.0 0.7 convolution_bitcast_fusion.7
  52.7 0.0 all-to-all-done
  52.7 5.9 %reshape.128 = bf16[2048,2,4,8]{3,2,1,0:T(4,128)(2,1)} reshape(bf16[16,2,4096]{2,1,0:T(2,128)(2,1)S(1)} %all-to-all-done) | data formatting | bytes 524288
  58.7 5.9 %copy.48 = f32[4,8,2,16,128]{4,1,2,3,0:T(8,128)S(1)} copy(bf16[4,8,2,16,128]{1,0,2,4,3:T(4,128)(2,1)} %bitcast.115) | data formatting | bytes 786432 | tf_op jit(solution)/shard_map/convert_element_type | solution.py:108
  64.6 0.9 fusion.8
  65.5 0.1 fusion.77
  65.6 2.1 %collective-permute-start.3 = (bf16[4,8,32,15]{3,1,2,0:T(8,128)(2,1)S(1)}, bf16[4,8,32,15]{3,1,2,0:T(8,128)(2,1)S(1)}, u32[]{:S(2)}, u32[]{:S(2)}) collective-permute-start(bf16[4,8,32,15]{3,1,2,0:T(8,128)(2,1)S(1)} %get-tuple-element.8), channel_id=1, source_target_pairs={{1,0},{2,1},{3,2},{4,3},{5,4},{6,5},{7,6},{8,7},{9,8},{10,9},{11,1... | collective-permute-start | bytes 92168 | tf_op jit(solution)/shard_map/ppermute | solution.py:23
  67.7 3.5 %collective-permute-start.2 = (bf16[4,8,32,15]{3,1,2,0:T(8,128)(2,1)S(1)}, bf16[4,8,32,15]{3,1,2,0:T(8,128)(2,1)S(1)}, u32[]{:S(2)}, u32[]{:S(2)}) collective-permute-start(bf16[4,8,32,15]{3,1,2,0:T(8,128)(2,1)S(1)} %get-tuple-element.7), channel_id=1, source_target_pairs={{0,1},{1,2},{2,3},{3,4},{4,5},{5,6},{6,7},{7,8},{8,9},{9,10},{10,1... | collective-permute-start | bytes 92168 | tf_op jit(solution)/shard_map/ppermute | solution.py:21
  71.2 0.4 convolution_bitcast_fusion.11
  71.6 0.1 copy.77
  71.7 1.6 %collective-permute-done.3 = bf16[4,8,32,15]{3,1,2,0:T(8,128)(2,1)S(1)} collective-permute-done((bf16[4,8,32,15]{3,1,2,0:T(8,128)(2,1)S(1)}, bf16[4,8,32,15]{3,1,2,0:T(8,128)(2,1)S(1)}, u32[]{:S(2)}, u32[]{:S(2)}) %collective-permute-start.3) | collective-permute-done | bytes 30752 | tf_op jit(solution)/shard_map/ppermute | solution.py:23
  73.3 1.2 %collective-permute-done.2 = bf16[4,8,32,15]{3,1,2,0:T(8,128)(2,1)S(1)} collective-permute-done((bf16[4,8,32,15]{3,1,2,0:T(8,128)(2,1)S(1)}, bf16[4,8,32,15]{3,1,2,0:T(8,128)(2,1)S(1)}, u32[]{:S(2)}, u32[]{:S(2)}) %collective-permute-start.2) | collective-permute-done | bytes 30752 | tf_op jit(solution)/shard_map/ppermute | solution.py:21
  74.5 0.3 pad_maximum_fusion.8
  74.8 0.6 convolution_bitcast_fusion.6
  75.4 0.7 convolution_bitcast_fusion.5
  76.1 0.8 fusion.10
  77.0 0.1 fusion.78
  77.1 1.9 %collective-permute-start.5 = (bf16[8,32,15]{2,1,0:T(8,128)(2,1)S(1)}, bf16[8,32,15]{2,1,0:T(8,128)(2,1)S(1)}, u32[]{:S(2)}, u32[]{:S(2)}) collective-permute-start(bf16[8,32,15]{2,1,0:T(8,128)(2,1)S(1)} %get-tuple-element.10), channel_id=1, source_target_pairs={{1,0},{2,1},{3,2},{4,3},{5,4},{6,5},{7,6},{8,7},{9,8},{10,9},{11,1... | collective-permute-start | bytes 23048 | tf_op jit(solution)/shard_map/ppermute | solution.py:23
  79.0 4.6 %collective-permute-start.4 = (bf16[8,32,15]{2,1,0:T(8,128)(2,1)S(1)}, bf16[8,32,15]{2,1,0:T(8,128)(2,1)S(1)}, u32[]{:S(2)}, u32[]{:S(2)}) collective-permute-start(bf16[8,32,15]{2,1,0:T(8,128)(2,1)S(1)} %get-tuple-element.9), channel_id=1, source_target_pairs={{0,1},{1,2},{2,3},{3,4},{4,5},{5,6},{6,7},{7,8},{8,9},{9,10},{10,1... | collective-permute-start | bytes 23048 | tf_op jit(solution)/shard_map/ppermute | solution.py:21
  83.6 0.0 collective-permute-done.5
  83.6 1.1 %collective-permute-done.4 = bf16[8,32,15]{2,1,0:T(8,128)(2,1)S(1)} collective-permute-done((bf16[8,32,15]{2,1,0:T(8,128)(2,1)S(1)}, bf16[8,32,15]{2,1,0:T(8,128)(2,1)S(1)}, u32[]{:S(2)}, u32[]{:S(2)}) %collective-permute-start.4) | collective-permute-done | bytes 7712 | tf_op jit(solution)/shard_map/ppermute | solution.py:21
  84.7 0.4 convolution_bitcast_fusion
  85.2 0.7 convolution_bitcast_fusion.4
  85.9 0.9 fusion.9
  86.8 0.1 fusion.76
  86.9 1.9 %collective-permute-start.7 = (bf16[4,8,32,15]{3,1,2,0:T(8,128)(2,1)S(1)}, bf16[4,8,32,15]{3,1,2,0:T(8,128)(2,1)S(1)}, u32[]{:S(2)}, u32[]{:S(2)}) collective-permute-start(bf16[4,8,32,15]{3,1,2,0:T(8,128)(2,1)S(1)} %get-tuple-element.6), channel_id=1, source_target_pairs={{1,0},{2,1},{3,2},{4,3},{5,4},{6,5},{7,6},{8,7},{9,8},{10,9},{11,1... | collective-permute-start | bytes 92168 | tf_op jit(solution)/shard_map/ppermute | solution.py:23
  88.8 4.3 %collective-permute-start.6 = (bf16[4,8,32,15]{3,1,2,0:T(8,128)(2,1)S(1)}, bf16[4,8,32,15]{3,1,2,0:T(8,128)(2,1)S(1)}, u32[]{:S(2)}, u32[]{:S(2)}) collective-permute-start(bf16[4,8,32,15]{3,1,2,0:T(8,128)(2,1)S(1)} %get-tuple-element.5), channel_id=1, source_target_pairs={{0,1},{1,2},{2,3},{3,4},{4,5},{5,6},{6,7},{7,8},{8,9},{9,10},{10,1... | collective-permute-start | bytes 92168 | tf_op jit(solution)/shard_map/ppermute | solution.py:21
  93.1 2.1 %collective-permute-done.7 = bf16[4,8,32,15]{3,1,2,0:T(8,128)(2,1)S(1)} collective-permute-done((bf16[4,8,32,15]{3,1,2,0:T(8,128)(2,1)S(1)}, bf16[4,8,32,15]{3,1,2,0:T(8,128)(2,1)S(1)}, u32[]{:S(2)}, u32[]{:S(2)}) %collective-permute-start.7) | collective-permute-done | bytes 30752 | tf_op jit(solution)/shard_map/ppermute | solution.py:23
  95.2 1.9 %collective-permute-done.6 = bf16[4,8,32,15]{3,1,2,0:T(8,128)(2,1)S(1)} collective-permute-done((bf16[4,8,32,15]{3,1,2,0:T(8,128)(2,1)S(1)}, bf16[4,8,32,15]{3,1,2,0:T(8,128)(2,1)S(1)}, u32[]{:S(2)}, u32[]{:S(2)}) %collective-permute-start.6) | collective-permute-done | bytes 30752 | tf_op jit(solution)/shard_map/ppermute | solution.py:21
  97.1 0.3 pad_maximum_fusion.9
  97.5 0.6 convolution_bitcast_fusion.3
  98.0 0.7 convolution_bitcast_fusion.2
  98.8 0.8 fusion.11
  99.6 0.7 fusion.46
  (11 shorter events, 0.1 us)
Async XLA Ops:
  6.3 13.8 %copy-start = (f32[8,32,128]{2,1,0:T(8,128)S(1)}, f32[8,32,128]{2,1,0:T(8,128)}, u32[]{:S(2)}) copy-start(f32[8,32,128]{2,1,0:T(8,128)} %param.6) | copy-start | bytes 393220
  6.3 19.6 %copy-start.1 = (f32[1,4,3,31]{3,1,2,0:T(4,128)S(1)}, f32[1,4,3,31]{3,1,2,0:T(4,128)}, u32[]{:S(2)}) copy-start(f32[1,4,3,31]{3,1,2,0:T(4,128)} %param.7) | copy-start | bytes 4468
  6.3 40.3 %copy-start.3 = (s32[16]{0:T(128)S(1)}, s32[16]{0:T(128)}, u32[]{:S(2)}) copy-start(s32[16]{0:T(128)} %param.8) | copy-start | bytes 196
  6.3 43.1 %copy-start.2 = (s32[16,4]{0,1:T(4,128)S(1)}, s32[16,4]{0,1:T(4,128)}, u32[]{:S(2)}) copy-start(s32[16,4]{0,1:T(4,128)} %param.9) | copy-start | bytes 772
  12.8 39.9 %all-to-all-start = ((bf16[16,2,4096]{2,1,0:T(2,128)(2,1)}), bf16[16,2,4096]{2,1,0:T(2,128)(2,1)S(1)}, u32[]{:S(2)}, u32[]{:S(2)}) async-start(bf16[16,2,4096]{2,1,0:T(2,128)(2,1)} %reshape.127), calls=%async_computation | async-start | bytes 524288 | tf_op jit(solution)/shard_map/all_to_all | solution.py:73
  20.3 31.2 %collective-permute-start.1 = (bf16[8,32,15]{2,1,0:T(8,128)(2,1)S(1)}, bf16[8,32,15]{2,1,0:T(8,128)(2,1)S(1)}, u32[]{:S(2)}, u32[]{:S(2)}) collective-permute-start(bf16[8,32,15]{2,1,0:T(8,128)(2,1)S(1)} %get-tuple-element.12), channel_id=1, source_target_pairs={{1,0},{2,1},{3,2},{4,3},{5,4},{6,5},{7,6},{8,7},{9,8},{10,9},{11,1... | collective-permute-start | bytes 23048 | tf_op jit(solution)/shard_map/ppermute | solution.py:23
  22.3 29.2 %collective-permute-start = (bf16[8,32,15]{2,1,0:T(8,128)(2,1)S(1)}, bf16[8,32,15]{2,1,0:T(8,128)(2,1)S(1)}, u32[]{:S(2)}, u32[]{:S(2)}) collective-permute-start(bf16[8,32,15]{2,1,0:T(8,128)(2,1)S(1)} %get-tuple-element.11), channel_id=1, source_target_pairs={{0,1},{1,2},{2,3},{3,4},{4,5},{5,6},{6,7},{7,8},{8,9},{9,10},{10,1... | collective-permute-start | bytes 23048 | tf_op jit(solution)/shard_map/ppermute | solution.py:21
  65.6 7.7 %collective-permute-start.3 = (bf16[4,8,32,15]{3,1,2,0:T(8,128)(2,1)S(1)}, bf16[4,8,32,15]{3,1,2,0:T(8,128)(2,1)S(1)}, u32[]{:S(2)}, u32[]{:S(2)}) collective-permute-start(bf16[4,8,32,15]{3,1,2,0:T(8,128)(2,1)S(1)} %get-tuple-element.8), channel_id=1, source_target_pairs={{1,0},{2,1},{3,2},{4,3},{5,4},{6,5},{7,6},{8,7},{9,8},{10,9},{11,1... | collective-permute-start | bytes 92168 | tf_op jit(solution)/shard_map/ppermute | solution.py:23
  67.7 6.8 %collective-permute-start.2 = (bf16[4,8,32,15]{3,1,2,0:T(8,128)(2,1)S(1)}, bf16[4,8,32,15]{3,1,2,0:T(8,128)(2,1)S(1)}, u32[]{:S(2)}, u32[]{:S(2)}) collective-permute-start(bf16[4,8,32,15]{3,1,2,0:T(8,128)(2,1)S(1)} %get-tuple-element.7), channel_id=1, source_target_pairs={{0,1},{1,2},{2,3},{3,4},{4,5},{5,6},{6,7},{7,8},{8,9},{9,10},{10,1... | collective-permute-start | bytes 92168 | tf_op jit(solution)/shard_map/ppermute | solution.py:21
  77.1 6.5 %collective-permute-start.5 = (bf16[8,32,15]{2,1,0:T(8,128)(2,1)S(1)}, bf16[8,32,15]{2,1,0:T(8,128)(2,1)S(1)}, u32[]{:S(2)}, u32[]{:S(2)}) collective-permute-start(bf16[8,32,15]{2,1,0:T(8,128)(2,1)S(1)} %get-tuple-element.10), channel_id=1, source_target_pairs={{1,0},{2,1},{3,2},{4,3},{5,4},{6,5},{7,6},{8,7},{9,8},{10,9},{11,1... | collective-permute-start | bytes 23048 | tf_op jit(solution)/shard_map/ppermute | solution.py:23
  79.0 5.7 %collective-permute-start.4 = (bf16[8,32,15]{2,1,0:T(8,128)(2,1)S(1)}, bf16[8,32,15]{2,1,0:T(8,128)(2,1)S(1)}, u32[]{:S(2)}, u32[]{:S(2)}) collective-permute-start(bf16[8,32,15]{2,1,0:T(8,128)(2,1)S(1)} %get-tuple-element.9), channel_id=1, source_target_pairs={{0,1},{1,2},{2,3},{3,4},{4,5},{5,6},{6,7},{7,8},{8,9},{9,10},{10,1... | collective-permute-start | bytes 23048 | tf_op jit(solution)/shard_map/ppermute | solution.py:21
  86.9 8.3 %collective-permute-start.7 = (bf16[4,8,32,15]{3,1,2,0:T(8,128)(2,1)S(1)}, bf16[4,8,32,15]{3,1,2,0:T(8,128)(2,1)S(1)}, u32[]{:S(2)}, u32[]{:S(2)}) collective-permute-start(bf16[4,8,32,15]{3,1,2,0:T(8,128)(2,1)S(1)} %get-tuple-element.6), channel_id=1, source_target_pairs={{1,0},{2,1},{3,2},{4,3},{5,4},{6,5},{7,6},{8,7},{9,8},{10,9},{11,1... | collective-permute-start | bytes 92168 | tf_op jit(solution)/shard_map/ppermute | solution.py:23
  88.8 8.3 %collective-permute-start.6 = (bf16[4,8,32,15]{3,1,2,0:T(8,128)(2,1)S(1)}, bf16[4,8,32,15]{3,1,2,0:T(8,128)(2,1)S(1)}, u32[]{:S(2)}, u32[]{:S(2)}) collective-permute-start(bf16[4,8,32,15]{3,1,2,0:T(8,128)(2,1)S(1)} %get-tuple-element.5), channel_id=1, source_target_pairs={{0,1},{1,2},{2,3},{3,4},{4,5},{5,6},{6,7},{7,8},{8,9},{9,10},{10,1... | collective-permute-start | bytes 92168 | tf_op jit(solution)/shard_map/ppermute | solution.py:21
where the time goes:
time: 101 us; the launch traced here: 100 us
  starting transfers between devices  31.2 us (31%)
  local copies, waits for them, and re-layouts  25.6 us (25%)
  blocking collectives  20.7 us (20%)
  matrix products  12.2 us (12%)
  waiting for transfers between devices  7.98 us (8%)
  other arithmetic  2.37 us (2%)
    all_gather x1, blocking collectives, shards(): fitted = lax.all_gather(psf_bank, ('plane', 'brick'), axis=0, tiled=True)  20.7 us
    unnamed x11, local copies, waits for them, and re-layouts  18.8 us
    ppermute x4, starting transfers between devices, padded_2(): lax.ppermute(tail, axis, [(i, (i + 1) % count) for i in range(ends)])  15.9 us
    ppermute x4, starting transfers between devices, padded_2(): lax.ppermute(head, axis, [((i + 1) % count, i) for i in range(ends)])  7.93 us
    all_to_all x1, starting transfers between devices, shards(): lax.all_to_all(camera_rows, ('plane', 'brick'), split_axis=3, concat_axis...  7.35 us
    convert_element_type x1, local copies, waits for them, and re-layouts, shards(): regrouped.astype(jnp.float32) / (blurred + BACKGROUND)  5.93 us
    ppermute x4, waiting for transfers between devices, padded_2(): lax.ppermute(tail, axis, [(i, (i + 1) % count) for i in range(ends)])  4.22 us
    ppermute x4, waiting for transfers between devices, padded_2(): lax.ppermute(head, axis, [((i + 1) % count, i) for i in range(ends)])  3.76 us
  transfers between devices with their start and end apart: 9, of which 5 were waited for; matrix products, arithmetic and copies ran while one was open for 7% of the time, Pallas kernels for 0%

commit v1 on v0

--- a/solution.py
+++ b/solution.py
@@ -8,6 +8,17 @@
 ITERS = 2
 BACKGROUND = 0.1
 HIGHEST = lax.Precision.HIGHEST
+
+
+def cut_along(x, dim, size):
+    before, after = (x.shape[:dim], x.shape[dim + 1 :])
+    return jnp.moveaxis(x.reshape(*before, size, -1, *after), dim, 0)
+
+
+def in_order(blocks, dim):
+    blocks = jnp.moveaxis(blocks, 0, dim)
+    lengths = blocks.shape
+    return blocks.reshape(*lengths[:dim], lengths[dim] * lengths[dim + 1], *lengths[dim + 2 :])
 
 
 def padded_2(cells, sides, width):
@@ -70,9 +81,16 @@
 
 
 def shards(camera_rows, estimate, psf_bank, psf_owner, view_mask):
-    regrouped = lax.all_to_all(
-        camera_rows, ("plane", "brick"), split_axis=3, concat_axis=2, tiled=True
-    )
+    size, place = (lax.axis_size(("plane", "brick")), lax.axis_index(("plane", "brick")))
+    tiles = cut_along(camera_rows, 3, size)
+    outs = [tiles[place]]
+    for step in range(1, size):
+        sent = tiles[place ^ step]
+        outs.append(
+            lax.ppermute(sent, ("plane", "brick"), [(i_2, i_2 ^ step) for i_2 in range(size)])
+        )
+    tiles = jnp.stack(outs)[place ^ jnp.arange(size)]
+    regrouped = in_order(tiles, 2)
     position = lax.axis_index(("plane", "brick"))
     brick_ids = jnp.arange(psf_owner.shape[0], dtype=jnp.int32)
     is_mine = brick_ids == position

time: 101 us -> 98.2 us (0.972)
  local copies, waits for them, and re-layouts: 25.6 us -> 3.61 us
  starting transfers between devices: 31.2 us -> 41.1 us
  waiting for transfers between devices: 7.98 us -> 15.4 us
  blocking collectives: 20.7 us -> 22.3 us
    ppermute x0 -> x15, starting transfers between devices: none -> 21.4 us  [shards(): lax.ppermute(sent, ('plane', 'brick'), [(i_2, i_2 ^ step) for i_2 in rang...]
    unnamed x11 -> x38, local copies, waits for them, and re-layouts: 18.8 us -> 0.23 us
    ppermute x4, waiting for transfers between devices: 3.76 us -> 12 us  [padded_2(): lax.ppermute(head, axis, [((i + 1) % count, i) for i in range(ends)])]
    all_to_all x1 -> x0, starting transfers between devices: 7.35 us -> none  [shards(): lax.all_to_all(camera_rows, ('plane', 'brick'), split_axis=3, concat_axis...]
    convert_element_type x1, local copies, waits for them, and re-layouts: 5.93 us -> 0.04 us  [shards(): regrouped.astype(jnp.float32) / (blurred + BACKGROUND)]
    ppermute x4, starting transfers between devices: 15.9 us -> 10.8 us  [padded_2(): lax.ppermute(tail, axis, [(i, (i + 1) % count) for i in range(ends)])]
    ppermute x4, waiting for transfers between devices: 4.22 us -> 1.77 us  [padded_2(): lax.ppermute(tail, axis, [(i, (i + 1) % count) for i in range(ends)])]
    ppermute x0 -> x15, waiting for transfers between devices: none -> 1.66 us  [shards(): lax.ppermute(sent, ('plane', 'brick'), [(i_2, i_2 ^ step) for i_2 in rang...]
  transfers between devices with their start and end apart: 9 -> 23, of which waited for: 5 -> 7; matrix products, arithmetic and copies ran while one was open for 7% -> 7% of each run, Pallas kernels for 0% -> 0%
where the time goes in v1:
time: 98.2 us; the launch traced here: 97.7 us
  starting transfers between devices  41.1 us (42%)
  blocking collectives  22.3 us (23%)
  waiting for transfers between devices  15.4 us (16%)
  matrix products  12.2 us (12%)
  local copies, waits for them, and re-layouts  3.61 us (4%)
  other arithmetic  2.43 us (2%)
    all_gather x1, blocking collectives, shards(): fitted = lax.all_gather(psf_bank, ('plane', 'brick'), axis=0, tiled=True)  22.3 us
    ppermute x15, starting transfers between devices, shards(): lax.ppermute(sent, ('plane', 'brick'), [(i_2, i_2 ^ step) for i_2 in rang...  21.4 us
    ppermute x4, waiting for transfers between devices, padded_2(): lax.ppermute(head, axis, [((i + 1) % count, i) for i in range(ends)])  12 us
    ppermute x4, starting transfers between devices, padded_2(): lax.ppermute(tail, axis, [(i, (i + 1) % count) for i in range(ends)])  10.8 us
    ppermute x4, starting transfers between devices, padded_2(): lax.ppermute(head, axis, [((i + 1) % count, i) for i in range(ends)])  8.84 us
    dot_general x4, matrix products, across_depth(): return jnp.einsum('vzyc,vzw->vwyc', volume, band_z, precision=HIGHEST)  3.35 us
    dot_general x6, matrix products, banded(): return jnp.einsum('ijt,vt->vij', one_hot, profiles, precision=HIGHEST)  3.14 us
    dot_general x4, matrix products, across_rows(): result = jnp.einsum('vzqic,vij->vzqjc', windows, band_y, precision=HIGHEST)  2.82 us
  transfers between devices with their start and end apart: 23, of which 7 were waited for; matrix products, arithmetic and copies ran while one was open for 7% of the time, Pallas kernels for 0%

profile of v1, /device:TPU:1, one launch (start us, length us, event | category | flops | bytes accessed | tf_op | source)
XLA Modules:
  0.0 97.7 jit_solution(2223158710586425879)
XLA Ops:
  0.0 1.1 %reshape.184 = bf16[4,8,2,16,128]{4,3,2,1,0:T(8,128)(2,1)S(1)} reshape(bf16[4,8,2,2048]{3,2,1,0:T(2,128)(2,1)} %param.5) | data formatting | bytes 524288 | tf_op jit(solution)/shard_map/reshape | solution.py:15
  1.2 0.7 constant_dynamic-slice_fusion
  2.0 0.1 collective-permute-start
  2.1 2.7 %collective-permute-start.1 = (bf16[4,8,2,128]{3,1,2,0:T(8,128)(2,1)S(1)}, bf16[4,8,2,128]{3,1,2,0:T(8,128)(2,1)S(1)}, u32[]{:S(2)}, u32[]{:S(2)}) collective-permute-start(bf16[4,8,2,128]{3,1,2,0:T(8,128)(2,1)S(1)} %bitcast.218), channel_id=1, source_target_pairs={{0,2},{1,3},{2,0},{3,1},{4,6},{5,7},{6,4},{7,5},{8,10},{9,11},{10,... | collective-permute-start | bytes 49160 | tf_op jit(solution)/shard_map/ppermute | solution.py:90
  4.8 0.0 collective-permute-start.2
  4.9 0.1 fusion.80
  5.0 3.6 %collective-permute-start.15 = (bf16[8,32,15]{2,1,0:T(8,128)(2,1)S(1)}, bf16[8,32,15]{2,1,0:T(8,128)(2,1)S(1)}, u32[]{:S(2)}, u32[]{:S(2)}) collective-permute-start(bf16[8,32,15]{2,1,0:T(8,128)(2,1)S(1)} %get-tuple-element.27), channel_id=1, source_target_pairs={{0,1},{1,2},{2,3},{3,4},{4,5},{5,6},{6,7},{7,8},{8,9},{9,10},{10,1... | collective-permute-start | bytes 23048 | tf_op jit(solution)/shard_map/ppermute | solution.py:32
  8.6 1.9 %collective-permute-start.16 = (bf16[8,32,15]{2,1,0:T(8,128)(2,1)S(1)}, bf16[8,32,15]{2,1,0:T(8,128)(2,1)S(1)}, u32[]{:S(2)}, u32[]{:S(2)}) collective-permute-start(bf16[8,32,15]{2,1,0:T(8,128)(2,1)S(1)} %get-tuple-element.28), channel_id=1, source_target_pairs={{1,0},{2,1},{3,2},{4,3},{5,4},{6,5},{7,6},{8,7},{9,8},{10,9},{11,1... | collective-permute-start | bytes 23048 | tf_op jit(solution)/shard_map/ppermute | solution.py:34
  10.6 0.6 select_reduce_fusion.1
  11.2 22.3 %all_gather.3 = f32[16,4,3,31]{3,1,2,0:T(4,128)S(1)} all-gather(f32[1,4,3,31]{3,1,2,0:T(4,128)S(1)} %copy-done.1), channel_id=1, replica_groups=mesh['slab'=2,'plane'=8,'brick'=2] {'plane','brick'}, dimensions={0}, use_global_device_ids=true | all-gather | bytes 25296 | tf_op jit(solution)/shard_map/all_gather | solution.py:99
  33.6 0.8 fusion.48
  34.4 0.1 bitcast_reduce_fusion
  34.4 0.1 bitcast_divide_fusion
  34.5 0.9 fusion.12
  35.4 0.3 convolution_bitcast_fusion.8
  35.7 0.4 convolution_bitcast_fusion.10
  36.1 0.1 select_reduce_fusion
  36.3 0.1 slice.54
  36.3 0.9 fusion.13
  37.3 0.1 slice.48
  37.3 0.3 convolution_bitcast_fusion.9
  37.8 0.1 copy.90
  37.9 0.1 slice.46
  38.0 1.8 %collective-permute-start.4 = (bf16[4,8,2,128]{3,1,2,0:T(8,128)(2,1)S(1)}, bf16[4,8,2,128]{3,1,2,0:T(8,128)(2,1)S(1)}, u32[]{:S(2)}, u32[]{:S(2)}) collective-permute-start(bf16[4,8,2,128]{3,1,2,0:T(8,128)(2,1)S(1)} %bitcast.223), channel_id=1, source_target_pairs={{0,5},{1,4},{2,7},{3,6},{4,1},{5,0},{6,3},{7,2},{8,13},{9,12},{10,... | collective-permute-start | bytes 49160 | tf_op jit(solution)/shard_map/ppermute | solution.py:90
  39.8 0.4 convolution_bitcast_fusion.1
  40.3 0.7 convolution_bitcast_fusion.7
  41.0 0.1 collective-permute-start.5
  41.1 2.6 %collective-permute-start.6 = (bf16[4,8,2,128]{3,1,2,0:T(8,128)(2,1)S(1)}, bf16[4,8,2,128]{3,1,2,0:T(8,128)(2,1)S(1)}, u32[]{:S(2)}, u32[]{:S(2)}) collective-permute-start(bf16[4,8,2,128]{3,1,2,0:T(8,128)(2,1)S(1)} %bitcast.221), channel_id=1, source_target_pairs={{0,7},{1,6},{2,5},{3,4},{4,3},{5,2},{6,1},{7,0},{8,15},{9,14},{10,... | collective-permute-start | bytes 49160 | tf_op jit(solution)/shard_map/ppermute | solution.py:90
  43.7 2.7 %collective-permute-start.8 = (bf16[4,8,2,128]{3,1,2,0:T(8,128)(2,1)S(1)}, bf16[4,8,2,128]{3,1,2,0:T(8,128)(2,1)S(1)}, u32[]{:S(2)}, u32[]{:S(2)}) collective-permute-start(bf16[4,8,2,128]{3,1,2,0:T(8,128)(2,1)S(1)} %bitcast.217), channel_id=1, source_target_pairs={{0,9},{1,8},{2,11},{3,10},{4,13},{5,12},{6,15},{7,14},{8,1},{9,0},... | collective-permute-start | bytes 49160 | tf_op jit(solution)/shard_map/ppermute | solution.py:90
  46.4 3.5 %collective-permute-start.10 = (bf16[4,8,2,128]{3,1,2,0:T(8,128)(2,1)S(1)}, bf16[4,8,2,128]{3,1,2,0:T(8,128)(2,1)S(1)}, u32[]{:S(2)}, u32[]{:S(2)}) collective-permute-start(bf16[4,8,2,128]{3,1,2,0:T(8,128)(2,1)S(1)} %bitcast.214), channel_id=1, source_target_pairs={{0,11},{1,10},{2,9},{3,8},{4,15},{5,14},{6,13},{7,12},{8,3},{9,2},... | collective-permute-start | bytes 49160 | tf_op jit(solution)/shard_map/ppermute | solution.py:90
  49.9 3.6 %collective-permute-start.12 = (bf16[4,8,2,128]{3,1,2,0:T(8,128)(2,1)S(1)}, bf16[4,8,2,128]{3,1,2,0:T(8,128)(2,1)S(1)}, u32[]{:S(2)}, u32[]{:S(2)}) collective-permute-start(bf16[4,8,2,128]{3,1,2,0:T(8,128)(2,1)S(1)} %bitcast.212), channel_id=1, source_target_pairs={{0,13},{1,12},{2,15},{3,14},{4,9},{5,8},{6,11},{7,10},{8,5},{9,4},... | collective-permute-start | bytes 49160 | tf_op jit(solution)/shard_map/ppermute | solution.py:90
  53.6 4.4 %collective-permute-start.14 = (bf16[4,8,2,128]{3,1,2,0:T(8,128)(2,1)S(1)}, bf16[4,8,2,128]{3,1,2,0:T(8,128)(2,1)S(1)}, u32[]{:S(2)}, u32[]{:S(2)}) collective-permute-start(bf16[4,8,2,128]{3,1,2,0:T(8,128)(2,1)S(1)} %bitcast.210), channel_id=1, source_target_pairs={{0,15},{1,14},{2,13},{3,12},{4,11},{5,10},{6,9},{7,8},{8,7},{9,6},... | collective-permute-start | bytes 49160 | tf_op jit(solution)/shard_map/ppermute | solution.py:90
  58.0 0.8 collective-permute-done.13
  58.8 0.8 collective-permute-done.14
  59.6 0.6 gather_fusion
  60.3 0.9 fusion.8
  61.2 0.1 fusion.78
  61.4 3.4 %collective-permute-start.17 = (bf16[4,8,32,15]{3,1,2,0:T(8,128)(2,1)S(1)}, bf16[4,8,32,15]{3,1,2,0:T(8,128)(2,1)S(1)}, u32[]{:S(2)}, u32[]{:S(2)}) collective-permute-start(bf16[4,8,32,15]{3,1,2,0:T(8,128)(2,1)S(1)} %get-tuple-element.7), channel_id=1, source_target_pairs={{0,1},{1,2},{2,3},{3,4},{4,5},{5,6},{6,7},{7,8},{8,9},{9,10},{10,1... | collective-permute-start | bytes 92168 | tf_op jit(solution)/shard_map/ppermute | solution.py:32
  64.7 1.9 %collective-permute-start.18 = (bf16[4,8,32,15]{3,1,2,0:T(8,128)(2,1)S(1)}, bf16[4,8,32,15]{3,1,2,0:T(8,128)(2,1)S(1)}, u32[]{:S(2)}, u32[]{:S(2)}) collective-permute-start(bf16[4,8,32,15]{3,1,2,0:T(8,128)(2,1)S(1)} %get-tuple-element.8), channel_id=1, source_target_pairs={{1,0},{2,1},{3,2},{4,3},{5,4},{6,5},{7,6},{8,7},{9,8},{10,9},{11,1... | collective-permute-start | bytes 92168 | tf_op jit(solution)/shard_map/ppermute | solution.py:34
  66.6 0.4 convolution_bitcast_fusion.11
  67.0 0.1 copy.93
  67.1 0.9 collective-permute-done.17
  68.0 4.4 %collective-permute-done.18 = bf16[4,8,32,15]{3,1,2,0:T(8,128)(2,1)S(1)} collective-permute-done((bf16[4,8,32,15]{3,1,2,0:T(8,128)(2,1)S(1)}, bf16[4,8,32,15]{3,1,2,0:T(8,128)(2,1)S(1)}, u32[]{:S(2)}, u32[]{:S(2)}) %collective-permute-start.18) | collective-permute-done | bytes 30752 | tf_op jit(solution)/shard_map/ppermute | solution.py:34
  72.4 0.3 pad_maximum_fusion.8
  72.7 0.6 convolution_bitcast_fusion.6
  73.3 0.7 convolution_bitcast_fusion.5
  74.0 0.8 fusion.10
  74.9 0.1 fusion.79
  75.0 1.9 %collective-permute-start.19 = (bf16[8,32,15]{2,1,0:T(8,128)(2,1)S(1)}, bf16[8,32,15]{2,1,0:T(8,128)(2,1)S(1)}, u32[]{:S(2)}, u32[]{:S(2)}) collective-permute-start(bf16[8,32,15]{2,1,0:T(8,128)(2,1)S(1)} %get-tuple-element.25), channel_id=1, source_target_pairs={{0,1},{1,2},{2,3},{3,4},{4,5},{5,6},{6,7},{7,8},{8,9},{9,10},{10,1... | collective-permute-start | bytes 23048 | tf_op jit(solution)/shard_map/ppermute | solution.py:32
  76.9 2.6 %collective-permute-start.20 = (bf16[8,32,15]{2,1,0:T(8,128)(2,1)S(1)}, bf16[8,32,15]{2,1,0:T(8,128)(2,1)S(1)}, u32[]{:S(2)}, u32[]{:S(2)}) collective-permute-start(bf16[8,32,15]{2,1,0:T(8,128)(2,1)S(1)} %get-tuple-element.26), channel_id=1, source_target_pairs={{1,0},{2,1},{3,2},{4,3},{5,4},{6,5},{7,6},{8,7},{9,8},{10,9},{11,1... | collective-permute-start | bytes 23048 | tf_op jit(solution)/shard_map/ppermute | solution.py:34
  79.5 3.0 %collective-permute-done.20 = bf16[8,32,15]{2,1,0:T(8,128)(2,1)S(1)} collective-permute-done((bf16[8,32,15]{2,1,0:T(8,128)(2,1)S(1)}, bf16[8,32,15]{2,1,0:T(8,128)(2,1)S(1)}, u32[]{:S(2)}, u32[]{:S(2)}) %collective-permute-start.20) | collective-permute-done | bytes 7712 | tf_op jit(solution)/shard_map/ppermute | solution.py:34
  82.5 0.4 convolution_bitcast_fusion
  83.0 0.7 convolution_bitcast_fusion.4
  83.7 0.9 fusion.9
  84.6 0.1 fusion.77
  84.7 1.9 %collective-permute-start.21 = (bf16[4,8,32,15]{3,1,2,0:T(8,128)(2,1)S(1)}, bf16[4,8,32,15]{3,1,2,0:T(8,128)(2,1)S(1)}, u32[]{:S(2)}, u32[]{:S(2)}) collective-permute-start(bf16[4,8,32,15]{3,1,2,0:T(8,128)(2,1)S(1)} %get-tuple-element.5), channel_id=1, source_target_pairs={{0,1},{1,2},{2,3},{3,4},{4,5},{5,6},{6,7},{7,8},{8,9},{9,10},{10,1... | collective-permute-start | bytes 92168 | tf_op jit(solution)/shard_map/ppermute | solution.py:32
  86.6 2.4 %collective-permute-start.22 = (bf16[4,8,32,15]{3,1,2,0:T(8,128)(2,1)S(1)}, bf16[4,8,32,15]{3,1,2,0:T(8,128)(2,1)S(1)}, u32[]{:S(2)}, u32[]{:S(2)}) collective-permute-start(bf16[4,8,32,15]{3,1,2,0:T(8,128)(2,1)S(1)} %get-tuple-element.6), channel_id=1, source_target_pairs={{1,0},{2,1},{3,2},{4,3},{5,4},{6,5},{7,6},{8,7},{9,8},{10,9},{11,1... | collective-permute-start | bytes 92168 | tf_op jit(solution)/shard_map/ppermute | solution.py:34
  89.0 0.9 collective-permute-done.21
  89.9 4.6 %collective-permute-done.22 = bf16[4,8,32,15]{3,1,2,0:T(8,128)(2,1)S(1)} collective-permute-done((bf16[4,8,32,15]{3,1,2,0:T(8,128)(2,1)S(1)}, bf16[4,8,32,15]{3,1,2,0:T(8,128)(2,1)S(1)}, u32[]{:S(2)}, u32[]{:S(2)}) %collective-permute-start.22) | collective-permute-done | bytes 30752 | tf_op jit(solution)/shard_map/ppermute | solution.py:34
  94.5 0.3 pad_maximum_fusion.9
  94.8 0.6 convolution_bitcast_fusion.3
  95.4 0.7 convolution_bitcast_fusion.2
  96.1 0.8 fusion.11
  96.9 0.7 fusion.46
  (73 shorter events, 0.5 us)
Async XLA Ops:
  1.2 3.6 %copy-start = (f32[8,32,128]{2,1,0:T(8,128)S(1)}, f32[8,32,128]{2,1,0:T(8,128)}, u32[]{:S(2)}) copy-start(f32[8,32,128]{2,1,0:T(8,128)} %param.6) | copy-start | bytes 393220
  1.9 8.7 %copy-start.3 = (s32[16]{0:T(128)S(1)}, s32[16]{0:T(128)}, u32[]{:S(2)}) copy-start(s32[16]{0:T(128)} %param.8) | copy-start | bytes 196
  1.9 9.3 %copy-start.1 = (f32[1,4,3,31]{3,1,2,0:T(4,128)S(1)}, f32[1,4,3,31]{3,1,2,0:T(4,128)}, u32[]{:S(2)}) copy-start(f32[1,4,3,31]{3,1,2,0:T(4,128)} %param.7) | copy-start | bytes 4468
  2.0 39.0 %collective-permute-start = (bf16[4,8,2,128]{3,1,2,0:T(8,128)(2,1)S(1)}, bf16[4,8,2,128]{3,1,2,0:T(8,128)(2,1)S(1)}, u32[]{:S(2)}, u32[]{:S(2)}) collective-permute-start(bf16[4,8,2,128]{3,1,2,0:T(8,128)(2,1)S(1)} %bitcast.219), channel_id=1, source_target_pairs={{0,1},{1,0},{2,3},{3,2},{4,5},{5,4},{6,7},{7,6},{8,9},{9,8},{10,11... | collective-permute-start | bytes 49160 | tf_op jit(solution)/shard_map/ppermute | solution.py:90
  2.1 39.0 %collective-permute-start.1 = (bf16[4,8,2,128]{3,1,2,0:T(8,128)(2,1)S(1)}, bf16[4,8,2,128]{3,1,2,0:T(8,128)(2,1)S(1)}, u32[]{:S(2)}, u32[]{:S(2)}) collective-permute-start(bf16[4,8,2,128]{3,1,2,0:T(8,128)(2,1)S(1)} %bitcast.218), channel_id=1, source_target_pairs={{0,2},{1,3},{2,0},{3,1},{4,6},{5,7},{6,4},{7,5},{8,10},{9,11},{10,... | collective-permute-start | bytes 49160 | tf_op jit(solution)/shard_map/ppermute | solution.py:90
  4.8 38.9 %collective-permute-start.2 = (bf16[4,8,2,128]{3,1,2,0:T(8,128)(2,1)S(1)}, bf16[4,8,2,128]{3,1,2,0:T(8,128)(2,1)S(1)}, u32[]{:S(2)}, u32[]{:S(2)}) collective-permute-start(bf16[4,8,2,128]{3,1,2,0:T(8,128)(2,1)S(1)} %bitcast.216), channel_id=1, source_target_pairs={{0,3},{1,2},{2,1},{3,0},{4,7},{5,6},{6,5},{7,4},{8,11},{9,10},{10,... | collective-permute-start | bytes 49160 | tf_op jit(solution)/shard_map/ppermute | solution.py:90
  5.0 33.0 %collective-permute-start.15 = (bf16[8,32,15]{2,1,0:T(8,128)(2,1)S(1)}, bf16[8,32,15]{2,1,0:T(8,128)(2,1)S(1)}, u32[]{:S(2)}, u32[]{:S(2)}) collective-permute-start(bf16[8,32,15]{2,1,0:T(8,128)(2,1)S(1)} %get-tuple-element.27), channel_id=1, source_target_pairs={{0,1},{1,2},{2,3},{3,4},{4,5},{5,6},{6,7},{7,8},{8,9},{9,10},{10,1... | collective-permute-start | bytes 23048 | tf_op jit(solution)/shard_map/ppermute | solution.py:32
  8.6 29.4 %collective-permute-start.16 = (bf16[8,32,15]{2,1,0:T(8,128)(2,1)S(1)}, bf16[8,32,15]{2,1,0:T(8,128)(2,1)S(1)}, u32[]{:S(2)}, u32[]{:S(2)}) collective-permute-start(bf16[8,32,15]{2,1,0:T(8,128)(2,1)S(1)} %get-tuple-element.28), channel_id=1, source_target_pairs={{1,0},{2,1},{3,2},{4,3},{5,4},{6,5},{7,6},{8,7},{9,8},{10,9},{11,1... | collective-permute-start | bytes 23048 | tf_op jit(solution)/shard_map/ppermute | solution.py:34
  10.6 25.5 %copy-start.2 = (s32[16,4]{0,1:T(4,128)S(1)}, s32[16,4]{0,1:T(4,128)}, u32[]{:S(2)}) copy-start(s32[16,4]{0,1:T(4,128)} %param.9) | copy-start | bytes 772
  38.0 5.7 %collective-permute-start.3 = (bf16[4,8,2,128]{3,1,2,0:T(8,128)(2,1)S(1)}, bf16[4,8,2,128]{3,1,2,0:T(8,128)(2,1)S(1)}, u32[]{:S(2)}, u32[]{:S(2)}) collective-permute-start(bf16[4,8,2,128]{3,1,2,0:T(8,128)(2,1)S(1)} %bitcast.224), channel_id=1, source_target_pairs={{0,4},{1,5},{2,6},{3,7},{4,0},{5,1},{6,2},{7,3},{8,12},{9,13},{10,... | collective-permute-start | bytes 49160 | tf_op jit(solution)/shard_map/ppermute | solution.py:90
  38.0 8.4 %collective-permute-start.4 = (bf16[4,8,2,128]{3,1,2,0:T(8,128)(2,1)S(1)}, bf16[4,8,2,128]{3,1,2,0:T(8,128)(2,1)S(1)}, u32[]{:S(2)}, u32[]{:S(2)}) collective-permute-start(bf16[4,8,2,128]{3,1,2,0:T(8,128)(2,1)S(1)} %bitcast.223), channel_id=1, source_target_pairs={{0,5},{1,4},{2,7},{3,6},{4,1},{5,0},{6,3},{7,2},{8,13},{9,12},{10,... | collective-permute-start | bytes 49160 | tf_op jit(solution)/shard_map/ppermute | solution.py:90
  41.0 5.4 %collective-permute-start.5 = (bf16[4,8,2,128]{3,1,2,0:T(8,128)(2,1)S(1)}, bf16[4,8,2,128]{3,1,2,0:T(8,128)(2,1)S(1)}, u32[]{:S(2)}, u32[]{:S(2)}) collective-permute-start(bf16[4,8,2,128]{3,1,2,0:T(8,128)(2,1)S(1)} %bitcast.222), channel_id=1, source_target_pairs={{0,6},{1,7},{2,4},{3,5},{4,2},{5,3},{6,0},{7,1},{8,14},{9,15},{10,... | collective-permute-start | bytes 49160 | tf_op jit(solution)/shard_map/ppermute | solution.py:90
  41.1 8.8 %collective-permute-start.6 = (bf16[4,8,2,128]{3,1,2,0:T(8,128)(2,1)S(1)}, bf16[4,8,2,128]{3,1,2,0:T(8,128)(2,1)S(1)}, u32[]{:S(2)}, u32[]{:S(2)}) collective-permute-start(bf16[4,8,2,128]{3,1,2,0:T(8,128)(2,1)S(1)} %bitcast.221), channel_id=1, source_target_pairs={{0,7},{1,6},{2,5},{3,4},{4,3},{5,2},{6,1},{7,0},{8,15},{9,14},{10,... | collective-permute-start | bytes 49160 | tf_op jit(solution)/shard_map/ppermute | solution.py:90
  43.7 6.3 %collective-permute-start.7 = (bf16[4,8,2,128]{3,1,2,0:T(8,128)(2,1)S(1)}, bf16[4,8,2,128]{3,1,2,0:T(8,128)(2,1)S(1)}, u32[]{:S(2)}, u32[]{:S(2)}) collective-permute-start(bf16[4,8,2,128]{3,1,2,0:T(8,128)(2,1)S(1)} %bitcast.220), channel_id=1, source_target_pairs={{0,8},{1,9},{2,10},{3,11},{4,12},{5,13},{6,14},{7,15},{8,0},{9,1},... | collective-permute-start | bytes 49160 | tf_op jit(solution)/shard_map/ppermute | solution.py:90
  43.7 9.8 %collective-permute-start.8 = (bf16[4,8,2,128]{3,1,2,0:T(8,128)(2,1)S(1)}, bf16[4,8,2,128]{3,1,2,0:T(8,128)(2,1)S(1)}, u32[]{:S(2)}, u32[]{:S(2)}) collective-permute-start(bf16[4,8,2,128]{3,1,2,0:T(8,128)(2,1)S(1)} %bitcast.217), channel_id=1, source_target_pairs={{0,9},{1,8},{2,11},{3,10},{4,13},{5,12},{6,15},{7,14},{8,1},{9,0},... | collective-permute-start | bytes 49160 | tf_op jit(solution)/shard_map/ppermute | solution.py:90
  46.4 7.2 %collective-permute-start.9 = (bf16[4,8,2,128]{3,1,2,0:T(8,128)(2,1)S(1)}, bf16[4,8,2,128]{3,1,2,0:T(8,128)(2,1)S(1)}, u32[]{:S(2)}, u32[]{:S(2)}) collective-permute-start(bf16[4,8,2,128]{3,1,2,0:T(8,128)(2,1)S(1)} %bitcast.215), channel_id=1, source_target_pairs={{0,10},{1,11},{2,8},{3,9},{4,14},{5,15},{6,12},{7,13},{8,2},{9,3},... | collective-permute-start | bytes 49160 | tf_op jit(solution)/shard_map/ppermute | solution.py:90
  46.4 11.5 %collective-permute-start.10 = (bf16[4,8,2,128]{3,1,2,0:T(8,128)(2,1)S(1)}, bf16[4,8,2,128]{3,1,2,0:T(8,128)(2,1)S(1)}, u32[]{:S(2)}, u32[]{:S(2)}) collective-permute-start(bf16[4,8,2,128]{3,1,2,0:T(8,128)(2,1)S(1)} %bitcast.214), channel_id=1, source_target_pairs={{0,11},{1,10},{2,9},{3,8},{4,15},{5,14},{6,13},{7,12},{8,3},{9,2},... | collective-permute-start | bytes 49160 | tf_op jit(solution)/shard_map/ppermute | solution.py:90
  49.9 8.0 %collective-permute-start.11 = (bf16[4,8,2,128]{3,1,2,0:T(8,128)(2,1)S(1)}, bf16[4,8,2,128]{3,1,2,0:T(8,128)(2,1)S(1)}, u32[]{:S(2)}, u32[]{:S(2)}) collective-permute-start(bf16[4,8,2,128]{3,1,2,0:T(8,128)(2,1)S(1)} %bitcast.213), channel_id=1, source_target_pairs={{0,12},{1,13},{2,14},{3,15},{4,8},{5,9},{6,10},{7,11},{8,4},{9,5},... | collective-permute-start | bytes 49160 | tf_op jit(solution)/shard_map/ppermute | solution.py:90
  49.9 8.0 %collective-permute-start.12 = (bf16[4,8,2,128]{3,1,2,0:T(8,128)(2,1)S(1)}, bf16[4,8,2,128]{3,1,2,0:T(8,128)(2,1)S(1)}, u32[]{:S(2)}, u32[]{:S(2)}) collective-permute-start(bf16[4,8,2,128]{3,1,2,0:T(8,128)(2,1)S(1)} %bitcast.212), channel_id=1, source_target_pairs={{0,13},{1,12},{2,15},{3,14},{4,9},{5,8},{6,11},{7,10},{8,5},{9,4},... | collective-permute-start | bytes 49160 | tf_op jit(solution)/shard_map/ppermute | solution.py:90
  53.5 5.3 %collective-permute-start.13 = (bf16[4,8,2,128]{3,1,2,0:T(8,128)(2,1)S(1)}, bf16[4,8,2,128]{3,1,2,0:T(8,128)(2,1)S(1)}, u32[]{:S(2)}, u32[]{:S(2)}) collective-permute-start(bf16[4,8,2,128]{3,1,2,0:T(8,128)(2,1)S(1)} %bitcast.211), channel_id=1, source_target_pairs={{0,14},{1,15},{2,12},{3,13},{4,10},{5,11},{6,8},{7,9},{8,6},{9,7},... | collective-permute-start | bytes 49160 | tf_op jit(solution)/shard_map/ppermute | solution.py:90
  53.6 6.1 %collective-permute-start.14 = (bf16[4,8,2,128]{3,1,2,0:T(8,128)(2,1)S(1)}, bf16[4,8,2,128]{3,1,2,0:T(8,128)(2,1)S(1)}, u32[]{:S(2)}, u32[]{:S(2)}) collective-permute-start(bf16[4,8,2,128]{3,1,2,0:T(8,128)(2,1)S(1)} %bitcast.210), channel_id=1, source_target_pairs={{0,15},{1,14},{2,13},{3,12},{4,11},{5,10},{6,9},{7,8},{8,7},{9,6},... | collective-permute-start | bytes 49160 | tf_op jit(solution)/shard_map/ppermute | solution.py:90
  61.4 6.7 %collective-permute-start.17 = (bf16[4,8,32,15]{3,1,2,0:T(8,128)(2,1)S(1)}, bf16[4,8,32,15]{3,1,2,0:T(8,128)(2,1)S(1)}, u32[]{:S(2)}, u32[]{:S(2)}) collective-permute-start(bf16[4,8,32,15]{3,1,2,0:T(8,128)(2,1)S(1)} %get-tuple-element.7), channel_id=1, source_target_pairs={{0,1},{1,2},{2,3},{3,4},{4,5},{5,6},{6,7},{7,8},{8,9},{9,10},{10,1... | collective-permute-start | bytes 92168 | tf_op jit(solution)/shard_map/ppermute | solution.py:32
  64.7 7.7 %collective-permute-start.18 = (bf16[4,8,32,15]{3,1,2,0:T(8,128)(2,1)S(1)}, bf16[4,8,32,15]{3,1,2,0:T(8,128)(2,1)S(1)}, u32[]{:S(2)}, u32[]{:S(2)}) collective-permute-start(bf16[4,8,32,15]{3,1,2,0:T(8,128)(2,1)S(1)} %get-tuple-element.8), channel_id=1, source_target_pairs={{1,0},{2,1},{3,2},{4,3},{5,4},{6,5},{7,6},{8,7},{9,8},{10,9},{11,1... | collective-permute-start | bytes 92168 | tf_op jit(solution)/shard_map/ppermute | solution.py:34
  75.0 4.5 %collective-permute-start.19 = (bf16[8,32,15]{2,1,0:T(8,128)(2,1)S(1)}, bf16[8,32,15]{2,1,0:T(8,128)(2,1)S(1)}, u32[]{:S(2)}, u32[]{:S(2)}) collective-permute-start(bf16[8,32,15]{2,1,0:T(8,128)(2,1)S(1)} %get-tuple-element.25), channel_id=1, source_target_pairs={{0,1},{1,2},{2,3},{3,4},{4,5},{5,6},{6,7},{7,8},{8,9},{9,10},{10,1... | collective-permute-start | bytes 23048 | tf_op jit(solution)/shard_map/ppermute | solution.py:32
  76.9 5.6 %collective-permute-start.20 = (bf16[8,32,15]{2,1,0:T(8,128)(2,1)S(1)}, bf16[8,32,15]{2,1,0:T(8,128)(2,1)S(1)}, u32[]{:S(2)}, u32[]{:S(2)}) collective-permute-start(bf16[8,32,15]{2,1,0:T(8,128)(2,1)S(1)} %get-tuple-element.26), channel_id=1, source_target_pairs={{1,0},{2,1},{3,2},{4,3},{5,4},{6,5},{7,6},{8,7},{9,8},{10,9},{11,1... | collective-permute-start | bytes 23048 | tf_op jit(solution)/shard_map/ppermute | solution.py:34
  84.7 5.2 %collective-permute-start.21 = (bf16[4,8,32,15]{3,1,2,0:T(8,128)(2,1)S(1)}, bf16[4,8,32,15]{3,1,2,0:T(8,128)(2,1)S(1)}, u32[]{:S(2)}, u32[]{:S(2)}) collective-permute-start(bf16[4,8,32,15]{3,1,2,0:T(8,128)(2,1)S(1)} %get-tuple-element.5), channel_id=1, source_target_pairs={{0,1},{1,2},{2,3},{3,4},{4,5},{5,6},{6,7},{7,8},{8,9},{9,10},{10,1... | collective-permute-start | bytes 92168 | tf_op jit(solution)/shard_map/ppermute | solution.py:32
  86.6 7.9 %collective-permute-start.22 = (bf16[4,8,32,15]{3,1,2,0:T(8,128)(2,1)S(1)}, bf16[4,8,32,15]{3,1,2,0:T(8,128)(2,1)S(1)}, u32[]{:S(2)}, u32[]{:S(2)}) collective-permute-start(bf16[4,8,32,15]{3,1,2,0:T(8,128)(2,1)S(1)} %get-tuple-element.6), channel_id=1, source_target_pairs={{1,0},{2,1},{3,2},{4,3},{5,4},{6,5},{7,6},{8,7},{9,8},{10,9},{11,1... | collective-permute-start | bytes 92168 | tf_op jit(solution)/shard_map/ppermute | solution.py:34
